TPU v7x, 256 devices: a whole 4x4x8 slice. The times are simulated.
256 devices in a mesh: xfer: 8 (over z), row: 8 (over y_hi, x), col: 4 (over y_lo, core).
Axes of the slice: x: 4, y: 4 (y_hi: 2, y_lo: 2; y = y_hi * 2 + y_lo), z: 8, core: 2. Of those that a mesh axis runs over, the one named last changes fastest.
Arguments:
- vertex: bfloat16 [8, 2, 3584, 3584], P('xfer', None, 'row', 'col'), may hold values from -6 to 6
- bubble: bfloat16 [8, 2, 3584], P('xfer', None, 'row'), may hold values from -0.0625 to 0.0625
- previous: bfloat16 [8, 2, 3584, 3584], P('xfer', None, 'row', 'col'), may hold values from -6 to 6
- cross_map: int32 [8, 64], replicated, may hold values from 0 to 7, as said below
Outputs:
- updated: bfloat16 [8, 2, 3584, 3584], P('xfer', None, 'row', 'col')
- crossed: bfloat16 [8, 2, 3584, 3584], P('xfer', None, 'row', 'col')
Inputs may be any that keep to these rules, and one draw needn't show every extreme that they name: For every block b, cross_map[:, b] names each of the 8 transfers once; for every transfer q and every r, the 8 entries cross_map[q, r * 8] to cross_map[q, r * 8 + 7] name each transfer once.
All inputs are finite; a program needn't handle non-finite values.
Results may differ from a plain program's by a relative error of at most 0.0044.
Values may be sent and summed in bfloat16 or wider, within the bound.
A program may use at most 128 MiB of HBM per device.

v0:
```python
import jax
import jax.numpy as jnp
from jax import lax
from jax.sharding import PartitionSpec as P


def shards(vertex, bubble, previous, cross_map):
    rows_here = vertex.shape[2]
    cols_here = vertex.shape[3]
    diag = bubble[0].astype(jnp.float32)
    prev = previous[0].astype(jnp.float32)
    first = diag[0][:, None]
    second = diag[1][:, None]
    bubbled = jnp.stack(
        [first * prev[0] - second * prev[1], first * prev[1] + second * prev[0]]
    ).astype(jnp.bfloat16)[None]
    panel = lax.all_gather(vertex, "col", axis=3, tiled=True)
    stacked = panel[0].reshape(2 * rows_here, panel.shape[3])
    piece = lax.all_gather(bubbled, "row", axis=2, tiled=True)
    joined = jnp.concatenate([piece[0, 0], piece[0, 1]], axis=1)
    total = jnp.dot(stacked, joined, preferred_element_type=jnp.float32)
    real = total[:rows_here, :cols_here] - total[rows_here:, cols_here:]
    imag = total[:rows_here, cols_here:] + total[rows_here:, :cols_here]
    updated = (vertex[0].astype(jnp.float32) + jnp.stack([real, imag])).astype(jnp.bfloat16)[None]
    groups = lax.axis_size("xfer")
    height = rows_here // groups
    mine = lax.axis_index("xfer")
    row_index = lax.axis_index("row")
    columns_map = lax.dynamic_slice_in_dim(cross_map, row_index * groups, groups, 1)
    sources = lax.dynamic_index_in_dim(columns_map, mine, 0, keepdims=False)
    everything = lax.all_gather(updated, "xfer", axis=0, tiled=True)
    blocked = everything.reshape(groups, 2, groups, height, cols_here)
    picked = blocked[sources, :, jnp.arange(groups, dtype=jnp.int32)]
    crossed = jnp.transpose(picked, (1, 0, 2, 3))
    crossed = crossed.reshape(1, 2, rows_here, cols_here)
    return (updated, crossed)


def solution(mesh):
    in_specs = (
        P("xfer", None, "row", "col"),
        P("xfer", None, "row"),
        P("xfer", None, "row", "col"),
        P(),
    )
    out_specs = (P("xfer", None, "row", "col"), P("xfer", None, "row", "col"))
    return jax.shard_map(shards, mesh=mesh, in_specs=in_specs, out_specs=out_specs, check_vma=False)
```

profile of v0, /device:TPU:1, one launch (start us, length us, event | category | flops | bytes accessed | tf_op | source)
XLA Modules:
  0.0 407.8 jit_solution(497566515039551264)
XLA Ops:
  7.2 0.0 all-gather.4.cloned.1.call-start
  7.2 0.8 fusion.17
  8.0 1.6 convert_element_type.26
  9.6 0.5 fusion.10
  10.1 1.3 pad_maximum_fusion
  11.4 0.0 all-gather.4.cloned.1.call-update
  11.4 0.0 all-gather.6.cloned.1.call-start
  11.5 0.7 all-gather.6.cloned.1.call-update
  12.2 0.0 all-gather.8.cloned.1.call-start
  12.2 157.6 %all-gather.4.cloned.1.call-done = bf16[1,2,3584,896]{3,2,1,0:T(8,128)(2,1)} async-done(((bf16[1,2,448,896]{3,2,1,0:T(8,128)(2,1)}), bf16[1,2,3584,896]{3,2,1,0:T(8,128)(2,1)}) %all-gather.4.cloned.1.call-update) | async-done | bytes 12845072 | tf_op jit(solution)/shard_map/all_gather | solution.py:19
  169.9 10.4 %slice_bitcast_fusion.1 = (bf16[3584,896]{1,0:T(8,128)(2,1)}, bf16[3584,896]{1,0:T(8,128)(2,1)}) fusion(bf16[1,2,3584,896]{3,2,1,0:T(8,128)(2,1)} %all-gather.4.cloned.1.call-done), kind=kLoop, calls=%fused_computation.6 | loop fusion | bytes 25690112 | tf_op jit(solution)/shard_map/squeeze | solution.py:20
  180.2 57.9 %all-gather.6.cloned.1.call-done = bf16[1,2,448,3584]{3,2,1,0:T(8,128)(2,1)} async-done(((bf16[1,2,448,896]{3,2,1,0:T(8,128)(2,1)}), bf16[1,2,448,3584]{3,2,1,0:T(8,128)(2,1)}) %all-gather.6.cloned.1.call-update) | async-done | bytes 6422544 | tf_op jit(solution)/shard_map/all_gather | solution.py:17
  238.1 16.9 %fusion.4 = f32[896,1792]{1,0:T(8,128)S(1)} fusion(bf16[896,3584]{1,0:T(8,128)(2,1)} %bitcast.52, bf16[3584,896]{1,0:T(8,128)(2,1)} %get-tuple-element.3, bf16[3584,896]{1,0:T(8,128)(2,1)} %get-tuple-element.2), kind=kOutput, calls=%fused_computation.7 | convolution fusion | flops 11534860288 | bytes 25690112 | tf_op jit(solution)/shard_map/dot_general | solution.py:21
  255.1 0.0 copy-start
  255.1 0.3 fusion.9
  255.4 1.1 copy-done
  256.5 1.5 fusion.7
  258.0 0.0 all-gather.8.cloned.1.call-update
  258.0 0.8 fusion.15
  258.8 135.8 %all-gather.8.cloned.1.call-done = bf16[8,2,448,896]{3,2,1,0:T(8,128)(2,1)} async-done(((bf16[1,2,448,896]{3,2,1,0:T(8,128)(2,1)}), bf16[8,2,448,896]{3,2,1,0:T(8,128)(2,1)}) %all-gather.8.cloned.1.call-update) | async-done | bytes 12845072 | tf_op jit(solution)/shard_map/all_gather | solution.py:31
  394.6 5.5 %gather_fusion = bf16[8,2,56,896]{3,2,1,0:T(8,128)(2,1)S(1)} fusion(bf16[8,2,8,56,896]{4,3,2,1,0:T(8,128)(2,1)} %bitcast.49, s32[8]{0:T(128)S(1)} %fusion.15), kind=kCustom, calls=%fused_computation | custom fusion | bytes 3211328 | tf_op jit(solution)/shard_map/gather | solution.py:33
  400.0 1.3 copy.7
Async XLA Ops:
  7.2 162.7 %all-gather.4.cloned.1.call-start = ((), (), s32[]{:S(2)}) async-start(), calls=%async_computation | async-start | bytes 14450688 | tf_op jit(solution)/shard_map/all_gather | solution.py:19
  11.4 226.7 %all-gather.6.cloned.1.call-start = ((), (), s32[]{:S(2)}) async-start(), calls=%async_computation.1 | async-start | bytes 8028160 | tf_op jit(solution)/shard_map/all_gather | solution.py:17
  12.2 382.4 %all-gather.8.cloned.1.call-start = ((), (), s32[]{:S(2)}) async-start(), calls=%async_computation.2 | async-start | bytes 14450688 | tf_op jit(solution)/shard_map/all_gather | solution.py:31
  255.1 1.4 copy-start
Sparse Core Ops, SparseCore 0:
  11.5 158.2 all-gather.3
  171.7 66.3 all-gather.5
  258.1 136.3 all-gather.7
where the time goes:
time: 408 us
  waiting for transfers between devices  352 us (86%)
  local copies, waits for them, and re-layouts  19 us (5%)
  matrix products  16.9 us (4%)
  between operations  13.8 us (3%)
  other arithmetic  5.98 us (1%)
    all_gather x1, waiting for transfers between devices, shards(): piece = lax.all_gather(bubbled, 'row', axis=2, tiled=True)  158 us
    all_gather x1, waiting for transfers between devices, shards(): everything = lax.all_gather(updated, 'xfer', axis=0, tiled=True)  136 us
    all_gather x1, waiting for transfers between devices, shards(): panel = lax.all_gather(vertex, 'col', axis=3, tiled=True)  57.9 us
    dot_general x1, matrix products, shards(): total = jnp.dot(stacked, joined, preferred_element_type=jnp.float32)  16.9 us
    squeeze x1, local copies, waits for them, and re-layouts, shards(): joined = jnp.concatenate([piece[0, 0], piece[0, 1]], axis=1)  10.4 us
  transfers between devices with their start and end apart: 3, of which 3 were waited for; matrix products, arithmetic and copies ran while one was open for 3% of the time, Pallas kernels for 0%

commit v1 on v0

v1 whole, which is shorter than its diff:
```python
import jax
import jax.numpy as jnp
from jax import lax
from jax.experimental import pallas as pl
from jax.experimental.pallas import tpu as pltpu
from jax.sharding import PartitionSpec as P

MESH = pl.DeviceIdType.MESH
CHUNKS = 7
W = 128
H = 448
D = 896
G = 8
T = 56
LAG = 2
LATE = 4
BF = jnp.bfloat16
F32 = jnp.float32


def kernel(
    vertex,
    bubble,
    previous,
    cmap,
    updated,
    crossed,
    panel,
    prev,
    bub,
    kept,
    part_out,
    part_in,
    turn,
    settled,
    cross_out,
    cross_in,
    load_sem,
    t1_s,
    t1_r,
    t2_s,
    t2_r,
    d1_s,
    d1_r,
    d2_s,
    d2_r,
    bx_s,
    bx_r,
    by_s,
    by_r,
    c_s,
    c_r,
    z_s,
    z_r,
):
    z = lax.axis_index("xfer")
    row = lax.axis_index("row")
    col = lax.axis_index("col")
    x = lax.rem(row, 4)
    yh = lax.div(row, 4)
    yl = lax.div(col, 2)
    core = lax.rem(col, 2)
    other = 1 - yh
    right = (z, yh * 4 + lax.rem(x + 1, 4), col)
    left = (z, yh * 4 + lax.rem(x + 3, 4), col)
    beside = (z, row, (1 - yl) * 2 + core)
    across = (z, other * 4 + x, (1 - yl) * 2 + core)
    sibling = (z, row, yl * 2 + 1 - core)
    partner = (z, other * 4 + x, col)
    own = jnp.where(yh == yl, yh, 2)

    def remote(src, dst, send, recv, device):
        return pltpu.make_async_remote_copy(
            src_ref=src, dst_ref=dst, send_sem=send, recv_sem=recv, device_id=device, device_id_type=MESH
        )

    load_a = pltpu.make_async_copy(vertex, panel.at[core, own], load_sem.at[0])
    load_p = pltpu.make_async_copy(previous, prev, load_sem.at[1])
    load_a.start()
    load_p.start()

    barrier = pltpu.get_barrier_semaphore()
    for device in (right, left, beside, across, sibling, partner):
        pl.semaphore_signal(barrier, inc=1, device_id=device, device_id_type=MESH)
    for step in range(1, G):
        pl.semaphore_signal(barrier, inc=1, device_id=(lax.rem(z + step, G), row, col), device_id_type=MESH)
    pl.semaphore_wait(barrier, 6 + G - 1)

    def t1(i):
        ref = panel.at[core, own, pl.ds(pl.multiple_of(i * W, W), W)]
        return remote(ref, ref, t1_s.at[i], t1_r.at[i], beside)

    def t1_arrives(i):
        slot = jnp.where(yh == yl, 2, yh)
        ref = panel.at[core, slot, pl.ds(pl.multiple_of(i * W, W), W)]
        return remote(ref, ref, t1_s.at[i], t1_r.at[i], beside)

    def t2(i):
        rows = pl.ds(pl.multiple_of(i * W, W), W)
        return remote(panel.at[core, 2, rows], panel.at[core, yh, rows], t2_s.at[i], t2_r.at[i], across)

    def t2_arrives(i):
        ref = panel.at[core, other, pl.ds(pl.multiple_of(i * W, W), W)]
        return remote(ref, ref, t2_s.at[i], t2_r.at[i], across)

    def d1(which):
        return remote(panel.at[which, yh], panel.at[which, yh], d1_s.at[0], d1_r.at[0], sibling)

    def d2(which, i):
        ref = panel.at[which, other, pl.ds(pl.multiple_of(i * W, W), W)]
        return remote(ref, ref, d2_s.at[i], d2_r.at[i], sibling)

    def bx(n, way):
        ref = bub.at[n, pl.ds(pl.multiple_of(x * H, H), H)]
        return remote(ref, ref, bx_s.at[way, n], bx_r.at[way, n], (right, left)[way])

    def bx_arrives(n, way):
        ref = bub.at[n, pl.ds(pl.multiple_of(lax.rem(x + (3, 1)[way], 4) * H, H), H)]
        return remote(ref, ref, bx_s.at[way, n], bx_r.at[way, n], (right, left)[way])

    def by(n, way):
        start = lax.rem(x + (3, 1)[way], 4) * H + way * (H // 2)
        ref = bub.at[n, pl.ds(pl.multiple_of(start, H // 2), H // 2)]
        return remote(ref, ref, by_s.at[way, n], by_r.at[way, n], (right, left)[way])

    def by_arrives(n, way):
        start = lax.rem(x + 2, 4) * H + way * (H // 2)
        ref = bub.at[n, pl.ds(pl.multiple_of(start, H // 2), H // 2)]
        return remote(ref, ref, by_s.at[way, n], by_r.at[way, n], (right, left)[way])

    def c(n):
        return remote(part_out.at[n], part_in.at[n], c_s.at[n], c_r.at[n], partner)

    def cross(n, step):
        device = (lax.rem(z + step, G), row, col)
        return remote(cross_out.at[n, step], cross_in.at[n, step], z_s.at[n, step], z_r.at[n, step], device)

    def loop(count, body):
        def run(i, carry):
            body(i)
            return carry

        lax.fori_loop(0, count, run, 0)

    load_a.wait()
    loop(CHUNKS, lambda i: t1(i).start())

    load_p.wait()
    diag = bubble[...].astype(F32)
    first = jnp.broadcast_to(diag[0:1, :], (W, H)).T
    second = jnp.broadcast_to(diag[1:2, :], (W, H)).T

    def make_bubbled(n):
        columns = pl.ds(pl.multiple_of(n * W, W), W)
        real = prev[pl.ds(0, H), columns].astype(F32)
        imag = prev[pl.ds(H, H), columns].astype(F32)
        rows = pl.ds(pl.multiple_of(x * H, H), H)
        bub[n, rows, pl.ds(0, W)] = (first * real - second * imag).astype(BF)
        bub[n, rows, pl.ds(W, W)] = (first * imag + second * real).astype(BF)
        bx(n, 0).start()
        bx(n, 1).start()

    loop(CHUNKS, make_bubbled)

    def relay(i):
        t1_arrives(i).wait_recv()
        t2(i).start()
        for way in (0, 1):
            bx_arrives(i, way).wait_recv()
            by(i, way).start()

    loop(CHUNKS, relay)
    d1(core).start()

    def share(i):
        t2_arrives(i).wait_recv()
        d2(core, i).start()

    loop(CHUNKS, share)
    d1(1 - core).wait_recv()
    loop(CHUNKS, lambda i: d2(1 - core, i).wait_recv())

    goes = []
    for step in range(G):
        target = lax.rem(z + step, G)
        index = jnp.int32(0)
        for block in range(G):
            index = jnp.where(cmap[target, row * G + block] == z, block, index)
        goes.append(index)
    comes = []
    for block in range(G):
        back = z - cmap[z, row * G + block]
        comes.append(jnp.where(back < 0, back + G, back))

    def product(n, slot):
        total = jnp.dot(panel[0, slot], bub[n, pl.ds(0, D)], preferred_element_type=F32)
        total = total + jnp.dot(panel[1, slot], bub[n, pl.ds(D, D)], preferred_element_type=F32)
        real = total[:H, :W] - total[H:, W:]
        imag = total[:H, W:] + total[H:, :W]
        return real, imag

    def multiply(n):
        for way in (0, 1):
            by_arrives(n, way).wait_recv()
        real, imag = product(n, other)
        part_out[n, pl.ds(0, H)] = real.astype(BF)
        part_out[n, pl.ds(H, H)] = imag.astype(BF)
        c(n).start()
        real, imag = product(n, yh)
        kept[n, pl.ds(0, H)] = real
        kept[n, pl.ds(H, H)] = imag

    def finish(n):
        c(n).wait_recv()
        columns = pl.ds(pl.multiple_of(n * W, W), W)
        value = panel[core, own, :, columns].astype(F32) + (kept[n] + part_in[n].astype(F32))
        updated[:, columns] = value.astype(BF)
        for block in range(G):
            low = value[block * T : block * T + T]
            high = value[H + block * T : H + block * T + T]
            turn[block] = jnp.concatenate([low, high], axis=0).astype(BF)
        for step in range(G):
            if step:
                cross_out[n, step] = turn[goes[step]]
                cross(n, step).start()
            else:
                cross_in[n, step] = turn[goes[step]]

    def place(n):
        for step in range(1, G):
            cross(n, step).wait_recv()
        columns = pl.ds(pl.multiple_of(n * W, W), W)
        settled[...] = cross_in[n]
        blocks = [settled[comes[block]].astype(F32) for block in range(G)]
        crossed[pl.ds(0, H), columns] = jnp.concatenate([b[:T] for b in blocks], axis=0).astype(BF)
        crossed[pl.ds(H, H), columns] = jnp.concatenate([b[T:] for b in blocks], axis=0).astype(BF)

    def step(n):
        @pl.when(n < CHUNKS)
        def _():
            multiply(n)

        @pl.when((n >= LAG) & (n < CHUNKS + LAG))
        def _():
            finish(n - LAG)

        @pl.when(n >= LATE)
        def _():
            place(n - LATE)

    loop(CHUNKS + LATE, step)

    d1(core).wait_send()

    def drain(i):
        t1(i).wait_send()
        t2(i).wait_send()
        d2(core, i).wait_send()
        for way in (0, 1):
            bx(i, way).wait_send()
            by(i, way).wait_send()
        c(i).wait_send()
        for step in range(1, G):
            cross(i, step).wait_send()

    loop(CHUNKS, drain)


def shards(vertex, bubble, previous, cross_map):
    dma = pltpu.SemaphoreType.DMA
    updated, crossed = pl.pallas_call(
        kernel,
        out_shape=[jax.ShapeDtypeStruct((D, D), BF)] * 2,
        in_specs=[
            pl.BlockSpec(memory_space=pl.ANY),
            pl.BlockSpec(memory_space=pltpu.VMEM),
            pl.BlockSpec(memory_space=pl.ANY),
            pl.BlockSpec(memory_space=pltpu.SMEM),
        ],
        out_specs=[pl.BlockSpec(memory_space=pltpu.VMEM)] * 2,
        scratch_shapes=[
            pltpu.VMEM((2, 3, D, D), BF),
            pltpu.VMEM((D, D), BF),
            pltpu.VMEM((CHUNKS, 4 * H, 2 * W), BF),
            pltpu.VMEM((CHUNKS, D, W), F32),
            pltpu.VMEM((CHUNKS, D, W), BF),
            pltpu.VMEM((CHUNKS, D, W), BF),
            pltpu.VMEM((G, 2 * T, W), BF),
            pltpu.VMEM((G, 2 * T, W), BF),
            pltpu.VMEM((CHUNKS, G, 2 * T, W), BF),
            pltpu.VMEM((CHUNKS, G, 2 * T, W), BF),
            dma((2,)),
            dma((CHUNKS,)),
            dma((CHUNKS,)),
            dma((CHUNKS,)),
            dma((CHUNKS,)),
            dma((1,)),
            dma((1,)),
            dma((CHUNKS,)),
            dma((CHUNKS,)),
            dma((2, CHUNKS)),
            dma((2, CHUNKS)),
            dma((2, CHUNKS)),
            dma((2, CHUNKS)),
            dma((CHUNKS,)),
            dma((CHUNKS,)),
            dma((CHUNKS, G)),
            dma((CHUNKS, G)),
        ],
        compiler_params=pltpu.CompilerParams(
            collective_id=0, has_side_effects=True, vmem_limit_bytes=56 * 2**20
        ),
        cost_estimate=pl.CostEstimate(flops=8 * H * 4 * D * D, bytes_accessed=8 * D * D, transcendentals=0),
    )(vertex.reshape(D, D), bubble.reshape(2, H), previous.reshape(D, D), cross_map)
    return updated.reshape(1, 2, H, D), crossed.reshape(1, 2, H, D)


def solution(mesh):
    in_specs = (
        P("xfer", None, "row", "col"),
        P("xfer", None, "row"),
        P("xfer", None, "row", "col"),
        P(),
    )
    out_specs = (P("xfer", None, "row", "col"), P("xfer", None, "row", "col"))
    return jax.shard_map(shards, mesh=mesh, in_specs=in_specs, out_specs=out_specs, check_vma=False)
```

time: 408 us -> 111 us (0.27)
  waiting for transfers between devices: 352 us -> 0 us
  Pallas kernels: 0 us -> 107 us
  matrix products: 16.9 us -> 0 us
  local copies, waits for them, and re-layouts: 19 us -> 3.98 us
  between operations: 13.8 us -> 0.65 us
  other arithmetic: 5.98 us -> 0 us
    all_gather x3 -> x0, waiting for transfers between devices: 351 us -> none  [the longest x1 158 us: shards(): piece = lax.all_gather(bubbled, 'row', axis=2, tiled=True)]
    pallas_call x0 -> x1, Pallas kernels: none -> 107 us  [shards(): pl.pallas_call(kernel, out_shape=[jax.ShapeDtypeStruct((D, D), BF)] * 2,...]
    dot_general x1 -> x0, matrix products: 16.9 us -> none  [shards(): total = jnp.dot(stacked, joined, preferred_element_type=jnp.float32)]
    squeeze x1 -> x0, local copies, waits for them, and re-layouts: 10.4 us -> none  [shards(): joined = jnp.concatenate([piece[0, 0], piece[0, 1]], axis=1)]
    gather x1 -> x0, local copies, waits for them, and re-layouts: 5.46 us -> none  [shards(): picked = blocked[sources, :, jnp.arange(groups, dtype=jnp.int32)]]
  transfers between devices with their start and end apart: 3 -> 0, of which waited for: 3 -> 0; matrix products, arithmetic and copies ran while one was open for 3% -> 0% of each run, Pallas kernels for 0% -> 0%
where the time goes in v1:
time: 111 us
  Pallas kernels  107 us (96%)
  local copies, waits for them, and re-layouts  3.98 us (4%)
    pallas_call x1, Pallas kernels, shards(): pl.pallas_call(kernel, out_shape=[jax.ShapeDtypeStruct((D, D), BF)] * 2,...  107 us
    unnamed x4, local copies, waits for them, and re-layouts  3.98 us

profile of v1, /device:TPU:1, one launch (start us, length us, event | category | flops | bytes accessed | tf_op | source)
XLA Modules:
  0.0 111.2 jit_solution(16016471346501127696)
XLA Ops:
  0.6 106.6 %shard_map.59 = (bf16[896,896]{1,0:T(8,128)(2,1)}, bf16[896,896]{1,0:T(8,128)(2,1)}) custom-call(bf16[896,896]{1,0:T(8,128)(2,1)} %bitcast.7, bf16[2,448]{1,0:T(2,128)(2,1)} %bitcast.9, bf16[896,896]{1,0:T(8,128)(2,1)} %bitcast.8, s32[8,64]{1,0:T(8,128)} %cmap.1), custom_call_target="tpu_custom_call" | custom-call | flops 11509170176 | bytes 6422528 | tf_op jit(solution)/shard_map/pallas_call | solution.py:271
  107.2 0.0 copy-start
  107.2 2.8 %copy.8 = bf16[1,2,448,896]{3,2,1,0:T(8,128)(2,1)} copy(bf16[1,2,448,896]{3,2,1,0:T(8,128)(2,1)} %bitcast.6) | data formatting | bytes 3211264
  110.0 0.0 copy-done
  110.0 1.2 %copy.9 = bf16[1,2,448,896]{3,2,1,0:T(8,128)(2,1)} copy(bf16[1,2,448,896]{3,2,1,0:T(8,128)(2,1)S(1)} %bitcast.5) | data formatting | bytes 3211264
Async XLA Ops:
  107.2 2.8 %copy-start = (bf16[896,896]{1,0:T(8,128)(2,1)S(1)}, bf16[896,896]{1,0:T(8,128)(2,1)}, u32[]{:S(2)}) copy-start(bf16[896,896]{1,0:T(8,128)(2,1)} %get-tuple-element.5) | copy-start | bytes 4816900

commit v2 on v1

v2 whole, which is shorter than its diff:
```python
import jax
import jax.numpy as jnp
from jax import lax
from jax.experimental import pallas as pl
from jax.experimental.pallas import tpu as pltpu
from jax.sharding import PartitionSpec as P

MESH = pl.DeviceIdType.MESH
CHUNKS = 7
W = 128
H = 448
D = 896
G = 8
T = 56
AHEAD = 3
PIECES = 14
R = 64
E = 8
GROUPS = ((0, 4), (4, 3))
BF = jnp.bfloat16
F32 = jnp.float32


def kernel(
    vertex,
    bubble,
    previous,
    cross_map,
    updated_out,
    crossed_out,
    updated,
    crossed,
    panel,
    raw,
    prev,
    diag,
    cmap,
    bub,
    kept,
    part_out,
    part_in,
    turn,
    settled,
    cross_out,
    cross_in,
    load_sem,
    store_sem,
    t1_s,
    t1_r,
    t2_s,
    t2_r,
    d1_s,
    d1_r,
    d2_s,
    d2_r,
    bx_s,
    bx_r,
    by_s,
    by_r,
    c_s,
    c_r,
    z_s,
    z_r,
    go,
):
    z = lax.axis_index("xfer")
    row = lax.axis_index("row")
    col = lax.axis_index("col")
    x = lax.rem(row, 4)
    yh = lax.div(row, 4)
    yl = lax.div(col, 2)
    core = lax.rem(col, 2)
    other = 1 - yh
    right = (z, yh * 4 + lax.rem(x + 1, 4), col)
    left = (z, yh * 4 + lax.rem(x + 3, 4), col)
    beside = (z, row, (1 - yl) * 2 + core)
    across = (z, other * 4 + x, (1 - yl) * 2 + core)
    sibling = (z, row, yl * 2 + 1 - core)
    partner = (z, other * 4 + x, col)
    own = jnp.where(yh == yl, yh, 2)

    def remote(src, dst, send, recv, device):
        return pltpu.make_async_remote_copy(
            src_ref=src, dst_ref=dst, send_sem=send, recv_sem=recv, device_id=device, device_id_type=MESH
        )

    load_a = pltpu.make_async_copy(vertex, raw, load_sem.at[0])
    load_p = pltpu.make_async_copy(previous, prev, load_sem.at[1])
    load_d = pltpu.make_async_copy(bubble, diag, load_sem.at[2])
    load_m = pltpu.make_async_copy(cross_map, cmap, load_sem.at[3])
    for load in (load_a, load_p, load_d, load_m):
        load.start()

    barrier = pltpu.get_barrier_semaphore()
    for device in (right, left, beside, across, sibling, partner):
        pl.semaphore_signal(barrier, inc=1, device_id=device, device_id_type=MESH)
    for step in range(1, G):
        pl.semaphore_signal(barrier, inc=1, device_id=(lax.rem(z + step, G), row, col), device_id_type=MESH)

    def half(which):
        return pl.ds(pl.multiple_of(which * D, D), D)

    def t1(i):
        ref = panel.at[own, pl.ds(pl.multiple_of(i * R, R), R), half(core)]
        return remote(ref, ref, t1_s.at[0], t1_r.at[i], beside)

    def t1_arrives(i):
        slot = jnp.where(yh == yl, 2, yh)
        ref = panel.at[slot, pl.ds(pl.multiple_of(i * R, R), R), half(core)]
        return remote(ref, ref, t1_s.at[0], t1_r.at[i], beside)

    def t2(i):
        rows = pl.ds(pl.multiple_of(i * R, R), R)
        return remote(panel.at[2, rows, half(core)], panel.at[yh, rows, half(core)], t2_s.at[0], t2_r.at[i], across)

    def t2_arrives(i):
        ref = panel.at[other, pl.ds(pl.multiple_of(i * R, R), R), half(core)]
        return remote(ref, ref, t2_s.at[0], t2_r.at[i], across)

    def group_rows(group):
        first, count = GROUPS[group]
        return pl.ds(first * W, count * W)

    def d1(which, group):
        ref = panel.at[yh, group_rows(group), half(which)]
        return remote(ref, ref, d1_s.at[0], d1_r.at[group], sibling)

    def d2(which, i):
        ref = panel.at[other, pl.ds(pl.multiple_of(i * W, W), W), half(which)]
        return remote(ref, ref, d2_s.at[0], d2_r.at[jnp.where(i < GROUPS[1][0], 0, 1)], sibling)

    def d2_arrives(group):
        ref = panel.at[other, group_rows(group), half(1 - core)]
        return remote(ref, ref, d2_s.at[0], d2_r.at[group], sibling)

    def bx(n, way):
        ref = bub.at[n, pl.ds(pl.multiple_of(x * H, H), H)]
        return remote(ref, ref, bx_s.at[way], bx_r.at[way, n], (right, left)[way])

    def bx_arrives(n, way):
        ref = bub.at[n, pl.ds(pl.multiple_of(lax.rem(x + (3, 1)[way], 4) * H, H), H)]
        return remote(ref, ref, bx_s.at[way], bx_r.at[way, n], (right, left)[way])

    def by(n, way):
        start = lax.rem(x + (3, 1)[way], 4) * H + way * (H // 2)
        ref = bub.at[n, pl.ds(pl.multiple_of(start, H // 2), H // 2)]
        return remote(ref, ref, by_s.at[way], by_r.at[way, n], (right, left)[way])

    def by_arrives(n, way):
        start = lax.rem(x + 2, 4) * H + way * (H // 2)
        ref = bub.at[n, pl.ds(pl.multiple_of(start, H // 2), H // 2)]
        return remote(ref, ref, by_s.at[way], by_r.at[way, n], (right, left)[way])

    def c(group, n):
        rows = group_rows(group)
        return remote(part_out.at[n, rows], part_in.at[n, rows], c_s.at[0], c_r.at[group, n], partner)

    def cross(group, n, step):
        first, count = GROUPS[group]
        rows = pl.ds(first * 2 * E, count * 2 * E)
        device = (lax.rem(z + step, G), row, col)
        return remote(
            cross_out.at[n, step, rows],
            cross_in.at[n, step, rows],
            z_s.at[0],
            z_r.at[group, n],
            device,
        )

    def cross_arrives(group, n):
        first, count = GROUPS[group]
        ref = cross_in.at[n, pl.ds(1, G - 1), pl.ds(first * 2 * E, count * 2 * E)]
        return remote(ref, ref, z_s.at[0], z_r.at[group, n], partner)

    def loop(count, body):
        def run(i, carry):
            body(i)
            return carry

        lax.fori_loop(0, count, run, 0)

    load_a.wait()

    def arrange(n):
        columns = pl.ds(pl.multiple_of(n * W, W), W)
        value = raw[:, columns].astype(F32)
        pieces = []
        for i in range(CHUNKS):
            for part in range(2):
                for block in range(G):
                    start = part * H + block * T + i * E
                    pieces.append(value[start : start + E])
        panel[own, :, pl.ds(pl.multiple_of(core * D + n * W, W), W)] = jnp.concatenate(pieces, axis=0).astype(BF)

    loop(CHUNKS, arrange)

    for load in (load_p, load_d, load_m):
        load.wait()
    first = jnp.broadcast_to(diag[0:1, :].astype(F32), (W, H)).T
    second = jnp.broadcast_to(diag[1:2, :].astype(F32), (W, H)).T

    def make_bubbled(n):
        columns = pl.ds(pl.multiple_of(n * W, W), W)
        real = prev[pl.ds(0, H), columns].astype(F32)
        imag = prev[pl.ds(H, H), columns].astype(F32)
        rows = pl.ds(pl.multiple_of(x * H, H), H)
        bub[n, rows, pl.ds(0, W)] = (first * real - second * imag).astype(BF)
        bub[n, rows, pl.ds(W, W)] = (first * imag + second * real).astype(BF)

    def send_bubbled(n):
        for way in (0, 1):
            bx(n, way).start()

    loop(CHUNKS, make_bubbled)
    pl.semaphore_wait(barrier, 6 + G - 1)
    loop(PIECES, lambda i: t1(i).start())

    @pl.when(yh != yl)
    def _():
        loop(PIECES, lambda i: t2(i).start())

    loop(AHEAD, send_bubbled)

    goes = []
    for step in range(G):
        target = lax.rem(z + step, G)
        index = jnp.int32(0)
        for block in range(G):
            index = jnp.where(cmap[target, row * G + block] == z, block, index)
        goes.append(index)
    comes = []
    for block in range(G):
        back = z - cmap[z, row * G + block]
        comes.append(jnp.where(back < 0, back + G, back))

    def product(group, n, slot, target):
        first, count = GROUPS[group]
        rows = group_rows(group)
        total = jnp.dot(panel[slot, rows], bub[n], preferred_element_type=F32)
        mid = W // 2
        for i in range(count):
            upper = total[i * W : i * W + mid]
            lower = total[i * W + mid : i * W + W]
            start = (first + i) * W
            target[n, pl.ds(start, mid)] = (upper[:, :W] - lower[:, W:]).astype(target.dtype)
            target[n, pl.ds(start + mid, mid)] = (upper[:, W:] + lower[:, :W]).astype(target.dtype)

    def multiply(group, n):
        product(group, n, other, part_out)
        product(group, n, yh, kept)
        c(group, n).start()

    def finish(group, n):
        first, count = GROUPS[group]
        rows = group_rows(group)
        columns = pl.ds(pl.multiple_of(core * D + n * W, W), W)
        c(group, n).wait_recv()
        value = panel[own, rows, columns].astype(F32) + (kept[n, rows] + part_in[n, rows].astype(F32))
        kept[n, rows] = value
        high = pl.ds(first * 2 * E, count * 2 * E)
        for block in range(G):
            pieces = []
            for i in range(count):
                for part in range(2):
                    start = i * W + part * (W // 2) + block * E
                    pieces.append(value[start : start + E])
            turn[block, high] = jnp.concatenate(pieces, axis=0).astype(BF)
        for step in range(G):
            if step:
                cross_out[n, step, high] = turn[goes[step], high]
                cross(group, n, step).start()
            else:
                cross_in[n, step, high] = turn[goes[step], high]

    def store(which, n):
        columns = pl.ds(pl.multiple_of(n * W, W), W)
        source = (updated, crossed)[which].at[:, columns]
        return pltpu.make_async_copy(source, (updated_out, crossed_out)[which].at[:, columns], store_sem.at[which])

    def write(n):
        columns = pl.ds(pl.multiple_of(n * W, W), W)
        value = kept[n]
        for part in range(2):
            pieces = []
            for block in range(G):
                for i in range(CHUNKS):
                    start = i * W + part * (W // 2) + block * E
                    pieces.append(value[start : start + E])
            updated[pl.ds(part * H, H), columns] = jnp.concatenate(pieces, axis=0).astype(BF)
        store(0, n).start()

    def place(n):
        columns = pl.ds(pl.multiple_of(n * W, W), W)
        for group in (0, 1):
            cross_arrives(group, n).wait_recv()
        settled[...] = cross_in[n]
        blocks = [settled[comes[block]].astype(F32) for block in range(G)]
        for part in range(2):
            pieces = []
            for block in range(G):
                for i in range(CHUNKS):
                    start = i * 2 * E + part * E
                    pieces.append(blocks[block][start : start + E])
            crossed[pl.ds(part * H, H), columns] = jnp.concatenate(pieces, axis=0).astype(BF)
        store(1, n).start()

    def relay_vertex(i):
        for piece in (2 * i, 2 * i + 1):
            t1_arrives(piece).wait_recv()

            @pl.when(yh == yl)
            def _(piece=piece):
                t2(piece).start()

    def relay_bubbled(n):
        for way in (0, 1):
            bx_arrives(n, way).wait_recv()
            by(n, way).start()

        @pl.when(n + AHEAD < CHUNKS)
        def _():
            send_bubbled(n + AHEAD)

    def share(i):
        for piece in (2 * i, 2 * i + 1):
            t2_arrives(piece).wait_recv()
        d2(core, i).start()

    def group_arrives(group):
        d1(1 - core, group).wait_recv()
        d2_arrives(group).wait_recv()

    def bubbled_arrives(n):
        for way in (0, 1):
            by_arrives(n, way).wait_recv()

    def early(n):
        bubbled_arrives(n)
        multiply(0, n)

    def gather(i):
        relay_vertex(i)

        @pl.when(i == 3)
        def _():
            d1(core, 0).start()

        @pl.when(i == 6)
        def _():
            d1(core, 1).start()
            early(2)

        @pl.when(i >= 1)
        def _():
            share(i - 1)
            relay_bubbled(i - 1)

        @pl.when(i == 4)
        def _():
            group_arrives(0)

        @pl.when((i == 4) | (i == 5))
        def _():
            early(i - 4)

    loop(CHUNKS, gather)
    share(CHUNKS - 1)

    @pl.when(yh == yl)
    def _():
        pl.semaphore_signal(go, inc=1, device_id=beside, device_id_type=MESH)

    loop(2, lambda n: finish(0, n))

    @pl.when(yh != yl)
    def _():
        pl.semaphore_wait(go, 1)

    early(3)

    def step(s):
        @pl.when(s == 0)
        def _():
            group_arrives(1)

        @pl.when(s == 1)
        def _():
            relay_bubbled(CHUNKS - 1)

        @pl.when(s < CHUNKS)
        def _():
            multiply(1, s)

        @pl.when((s >= 1) & (s < 4))
        def _():
            early(s + 3)

        @pl.when((s < 2) | ((s >= 3) & (s < 6)))
        def _():
            finish(0, jnp.where(s < 2, s + 2, s + 1))

        @pl.when((s >= 2) & (s < CHUNKS + 2))
        def _():
            finish(1, s - 2)
            write(s - 2)

        @pl.when(s >= 5)
        def _():
            place(s - 5)

    loop(CHUNKS + 5, step)

    def sent(ref, semaphore):
        remote(ref, ref, semaphore, load_sem.at[0], partner).wait_send()

    sent(panel.at[own, :, half(core)], t1_s.at[0])
    sent(panel.at[2, :, half(core)], t2_s.at[0])
    sent(panel.at[yh, :, half(core)], d1_s.at[0])
    sent(panel.at[other, :, half(core)], d2_s.at[0])
    for way in (0, 1):
        sent(bub.at[:, pl.ds(pl.multiple_of(x * H, H), H)], bx_s.at[way])
        start = lax.rem(x + (3, 1)[way], 4) * H + way * (H // 2)
        sent(bub.at[:, pl.ds(pl.multiple_of(start, H // 2), H // 2)], by_s.at[way])
    sent(part_out, c_s.at[0])
    sent(cross_out.at[:, pl.ds(1, G - 1)], z_s.at[0])
    for which in (0, 1):
        source, target = ((updated, updated_out), (crossed, crossed_out))[which]
        pltpu.make_async_copy(source, target, store_sem.at[which]).wait()


def shards(vertex, bubble, previous, cross_map):
    dma = pltpu.SemaphoreType.DMA
    updated, crossed = pl.pallas_call(
        kernel,
        out_shape=[pltpu.VMEM((D, D), BF)] * 2,
        in_specs=[
            pl.BlockSpec(memory_space=pltpu.HBM),
            pl.BlockSpec(memory_space=pltpu.HBM),
            pl.BlockSpec(memory_space=pltpu.HBM),
            pl.BlockSpec(memory_space=pltpu.HBM),
        ],
        out_specs=[pl.BlockSpec(memory_space=pl.ANY)] * 2,
        scratch_shapes=[
            pltpu.VMEM((D, D), BF),
            pltpu.VMEM((D, D), BF),
            pltpu.VMEM((3, D, 2 * D), BF),
            pltpu.VMEM((D, D), BF),
            pltpu.VMEM((D, D), BF),
            pltpu.VMEM((2, H), BF),
            pltpu.SMEM((G, G * G), jnp.int32),
            pltpu.VMEM((CHUNKS, 4 * H, 2 * W), BF),
            pltpu.VMEM((CHUNKS, D, W), F32),
            pltpu.VMEM((CHUNKS, D, W), BF),
            pltpu.VMEM((CHUNKS, D, W), BF),
            pltpu.VMEM((G, 2 * T, W), BF),
            pltpu.VMEM((G, 2 * T, W), BF),
            pltpu.VMEM((CHUNKS, G, 2 * T, W), BF),
            pltpu.VMEM((CHUNKS, G, 2 * T, W), BF),
            dma((4,)),
            dma((2,)),
            dma((1,)),
            dma((PIECES,)),
            dma((1,)),
            dma((PIECES,)),
            dma((1,)),
            dma((2,)),
            dma((1,)),
            dma((2,)),
            dma((2,)),
            dma((2, CHUNKS)),
            dma((2,)),
            dma((2, CHUNKS)),
            dma((1,)),
            dma((2, CHUNKS)),
            dma((1,)),
            dma((2, CHUNKS)),
            pltpu.SemaphoreType.REGULAR,
        ],
        compiler_params=pltpu.CompilerParams(
            collective_id=0, has_side_effects=True, vmem_limit_bytes=60 * 2**20
        ),
        cost_estimate=pl.CostEstimate(flops=8 * H * 4 * D * D, bytes_accessed=8 * D * D, transcendentals=0),
    )(vertex.reshape(D, D), bubble.reshape(2, H), previous.reshape(D, D), cross_map)
    return updated.reshape(1, 2, H, D), crossed.reshape(1, 2, H, D)


def solution(mesh):
    in_specs = (
        P("xfer", None, "row", "col"),
        P("xfer", None, "row"),
        P("xfer", None, "row", "col"),
        P(),
    )
    out_specs = (P("xfer", None, "row", "col"), P("xfer", None, "row", "col"))
    return jax.shard_map(shards, mesh=mesh, in_specs=in_specs, out_specs=out_specs, check_vma=False)
```

time: 111 us -> 102 us (0.919); the launches traced: 111 us -> 100 us
  Pallas kernels: 107 us -> 97.4 us
  local copies, waits for them, and re-layouts: 3.98 us -> 2.31 us
    pallas_call x1, Pallas kernels: 107 us -> 97.4 us  [shards(): pl.pallas_call(kernel, out_shape=[pltpu.VMEM((D, D), BF)] * 2, in_specs=[...]
    unnamed x4 -> x2, local copies, waits for them, and re-layouts: 3.98 us -> 2.31 us
where the time goes in v2:
time: 102 us; the launch traced here: 100 us
  Pallas kernels  97.4 us (95%)
  local copies, waits for them, and re-layouts  2.31 us (2%)
    pallas_call x1, Pallas kernels, shards(): pl.pallas_call(kernel, out_shape=[pltpu.VMEM((D, D), BF)] * 2, in_specs=[...  97.4 us
    unnamed x2, local copies, waits for them, and re-layouts  2.31 us

profile of v2, /device:TPU:1, one launch (start us, length us, event | category | flops | bytes accessed | tf_op | source)
XLA Modules:
  0.0 100.4 jit_solution(9927729213988266036)
XLA Ops:
  0.6 97.4 %shard_map.59 = (bf16[896,896]{1,0:T(8,128)(2,1)S(1)}, bf16[896,896]{1,0:T(8,128)(2,1)S(1)}) custom-call(bf16[896,896]{1,0:T(8,128)(2,1)} %bitcast.7, bf16[2,448]{1,0:T(2,128)(2,1)} %bitcast.9, bf16[896,896]{1,0:T(8,128)(2,1)} %bitcast.8, s32[8,64]{1,0:T(8,128)} %cross_map.1), custom_call_target="tpu_custom_call" | custom-call | flops 11509170176 | bytes 6422528 | tf_op jit(solution)/shard_map/pallas_call | solution.py:433
  98.1 1.2 %copy.8 = bf16[1,2,448,896]{3,2,1,0:T(8,128)(2,1)} copy(bf16[1,2,448,896]{3,2,1,0:T(8,128)(2,1)S(1)} %bitcast.6) | data formatting | bytes 3211264
  99.2 1.2 %copy.9 = bf16[1,2,448,896]{3,2,1,0:T(8,128)(2,1)} copy(bf16[1,2,448,896]{3,2,1,0:T(8,128)(2,1)S(1)} %bitcast.5) | data formatting | bytes 3211264

commit v3 on v2

--- a/solution.py
+++ b/solution.py
@@ -12,9 +12,8 @@
 D = 896
 G = 8
 T = 56
-AHEAD = 3
-PIECES = 14
-R = 64
+HELD = 3
+AHEAD = 2
 E = 8
 GROUPS = ((0, 4), (4, 3))
 BF = jnp.bfloat16
@@ -31,6 +30,7 @@
     updated,
     crossed,
     panel,
+    mine,
     raw,
     prev,
     diag,
@@ -45,14 +45,11 @@
     cross_in,
     load_sem,
     store_sem,
-    t1_s,
+    t_s,
     t1_r,
-    t2_s,
     t2_r,
-    d1_s,
-    d1_r,
-    d2_s,
-    d2_r,
+    d_s,
+    d_r,
     bx_s,
     bx_r,
     by_s,
@@ -77,7 +74,7 @@
     across = (z, other * 4 + x, (1 - yl) * 2 + core)
     sibling = (z, row, yl * 2 + 1 - core)
     partner = (z, other * 4 + x, col)
-    own = jnp.where(yh == yl, yh, 2)
+    end = yh == yl
 
     def remote(src, dst, send, recv, device):
         return pltpu.make_async_remote_copy(
@@ -88,8 +85,7 @@
     load_p = pltpu.make_async_copy(previous, prev, load_sem.at[1])
     load_d = pltpu.make_async_copy(bubble, diag, load_sem.at[2])
     load_m = pltpu.make_async_copy(cross_map, cmap, load_sem.at[3])
-    for load in (load_a, load_p, load_d, load_m):
-        load.start()
+    load_a.start()
 
     barrier = pltpu.get_barrier_semaphore()
     for device in (right, left, beside, across, sibling, partner):
@@ -100,38 +96,43 @@
     def half(which):
         return pl.ds(pl.multiple_of(which * D, D), D)
 
-    def t1(i):
-        ref = panel.at[own, pl.ds(pl.multiple_of(i * R, R), R), half(core)]
-        return remote(ref, ref, t1_s.at[0], t1_r.at[i], beside)
+    def row_chunk(i):
+        return pl.ds(pl.multiple_of(i * W, W), W)
+
+    def t_end(i):
+        rows = row_chunk(i)
+        return remote(mine.at[rows], panel.at[yh, rows, half(core)], t_s.at[0], t1_r.at[i], beside)
+
+    def t_middle(i):
+        rows = row_chunk(i)
+        return remote(mine.at[rows], panel.at[yh, rows, half(core)], t_s.at[0], t2_r.at[i], across)
+
+    def t_far(i):
+        rows = row_chunk(i)
+        return remote(mine.at[rows], panel.at[yh, rows, half(core)], t_s.at[1], t2_r.at[i], partner)
 
     def t1_arrives(i):
-        slot = jnp.where(yh == yl, 2, yh)
-        ref = panel.at[slot, pl.ds(pl.multiple_of(i * R, R), R), half(core)]
-        return remote(ref, ref, t1_s.at[0], t1_r.at[i], beside)
-
-    def t2(i):
-        rows = pl.ds(pl.multiple_of(i * R, R), R)
-        return remote(panel.at[2, rows, half(core)], panel.at[yh, rows, half(core)], t2_s.at[0], t2_r.at[i], across)
+        ref = panel.at[yh, row_chunk(i), half(core)]
+        return remote(ref, ref, t_s.at[0], t1_r.at[i], beside)
 
     def t2_arrives(i):
-        ref = panel.at[other, pl.ds(pl.multiple_of(i * R, R), R), half(core)]
-        return remote(ref, ref, t2_s.at[0], t2_r.at[i], across)
+        ref = panel.at[other, row_chunk(i), half(core)]
+        return remote(ref, ref, t_s.at[0], t2_r.at[i], across)
+
+    def group_of(i):
+        return jnp.where(i < GROUPS[1][0], 0, 1)
 
     def group_rows(group):
         first, count = GROUPS[group]
         return pl.ds(first * W, count * W)
 
-    def d1(which, group):
-        ref = panel.at[yh, group_rows(group), half(which)]
-        return remote(ref, ref, d1_s.at[0], d1_r.at[group], sibling)
-
-    def d2(which, i):
-        ref = panel.at[other, pl.ds(pl.multiple_of(i * W, W), W), half(which)]
-        return remote(ref, ref, d2_s.at[0], d2_r.at[jnp.where(i < GROUPS[1][0], 0, 1)], sibling)
-
-    def d2_arrives(group):
-        ref = panel.at[other, group_rows(group), half(1 - core)]
-        return remote(ref, ref, d2_s.at[0], d2_r.at[group], sibling)
+    def share(slot, i):
+        ref = panel.at[slot, row_chunk(i), half(core)]
+        return remote(ref, ref, d_s.at[0], d_r.at[jnp.where(slot == yh, 0, 1), group_of(i)], sibling)
+
+    def share_arrives(slot, group):
+        ref = panel.at[slot, group_rows(group), half(1 - core)]
+        return remote(ref, ref, d_s.at[0], d_r.at[jnp.where(slot == yh, 0, 1), group], sibling)
 
     def bx(n, way):
         ref = bub.at[n, pl.ds(pl.multiple_of(x * H, H), H)]
@@ -180,6 +181,8 @@
         lax.fori_loop(0, count, run, 0)
 
     load_a.wait()
+    for load in (load_p, load_d, load_m):
+        load.start()
 
     def arrange(n):
         columns = pl.ds(pl.multiple_of(n * W, W), W)
@@ -190,9 +193,25 @@
                 for block in range(G):
                     start = part * H + block * T + i * E
                     pieces.append(value[start : start + E])
-        panel[own, :, pl.ds(pl.multiple_of(core * D + n * W, W), W)] = jnp.concatenate(pieces, axis=0).astype(BF)
+        ordered = jnp.concatenate(pieces, axis=0).astype(BF)
+        mine[:, columns] = ordered
+
+        @pl.when(end)
+        def _():
+            panel[yh, :, pl.ds(pl.multiple_of(core * D + n * W, W), W)] = ordered
 
     loop(CHUNKS, arrange)
+    pl.semaphore_wait(barrier, 6 + G - 1)
+
+    @pl.when(end)
+    def _():
+        loop(CHUNKS, lambda i: t_end(i).start())
+        loop(CHUNKS, lambda i: share(yh, i).start())
+
+    @pl.when(jnp.logical_not(end))
+    def _():
+        loop(CHUNKS, lambda i: t_far(i).start())
+        loop(CHUNKS, lambda i: t_middle(i).start())
 
     for load in (load_p, load_d, load_m):
         load.wait()
@@ -211,15 +230,12 @@
         for way in (0, 1):
             bx(n, way).start()
 
-    loop(CHUNKS, make_bubbled)
-    pl.semaphore_wait(barrier, 6 + G - 1)
-    loop(PIECES, lambda i: t1(i).start())
-
-    @pl.when(yh != yl)
-    def _():
-        loop(PIECES, lambda i: t2(i).start())
-
-    loop(AHEAD, send_bubbled)
+    def first_bubbled(n):
+        make_bubbled(n)
+        send_bubbled(n)
+
+    loop(AHEAD, first_bubbled)
+    loop(CHUNKS - AHEAD, lambda n: make_bubbled(n + AHEAD))
 
     goes = []
     for step in range(G):
@@ -248,14 +264,21 @@
     def multiply(group, n):
         product(group, n, other, part_out)
         product(group, n, yh, kept)
-        c(group, n).start()
+        if group:
+            c(group, n).start()
+        else:
+
+            @pl.when(jnp.logical_not(end) | (n >= HELD))
+            def _():
+                c(group, n).start()
+
 
     def finish(group, n):
         first, count = GROUPS[group]
         rows = group_rows(group)
-        columns = pl.ds(pl.multiple_of(core * D + n * W, W), W)
+        columns = pl.ds(pl.multiple_of(n * W, W), W)
         c(group, n).wait_recv()
-        value = panel[own, rows, columns].astype(F32) + (kept[n, rows] + part_in[n, rows].astype(F32))
+        value = mine[rows, columns].astype(F32) + (kept[n, rows] + part_in[n, rows].astype(F32))
         kept[n, rows] = value
         high = pl.ds(first * 2 * E, count * 2 * E)
         for block in range(G):
@@ -304,14 +327,6 @@
             crossed[pl.ds(part * H, H), columns] = jnp.concatenate(pieces, axis=0).astype(BF)
         store(1, n).start()
 
-    def relay_vertex(i):
-        for piece in (2 * i, 2 * i + 1):
-            t1_arrives(piece).wait_recv()
-
-            @pl.when(yh == yl)
-            def _(piece=piece):
-                t2(piece).start()
-
     def relay_bubbled(n):
         for way in (0, 1):
             bx_arrives(n, way).wait_recv()
@@ -321,14 +336,9 @@
         def _():
             send_bubbled(n + AHEAD)
 
-    def share(i):
-        for piece in (2 * i, 2 * i + 1):
-            t2_arrives(piece).wait_recv()
-        d2(core, i).start()
-
     def group_arrives(group):
-        d1(1 - core, group).wait_recv()
-        d2_arrives(group).wait_recv()
+        share_arrives(yh, group).wait_recv()
+        share_arrives(other, group).wait_recv()
 
     def bubbled_arrives(n):
         for way in (0, 1):
@@ -338,85 +348,95 @@
         bubbled_arrives(n)
         multiply(0, n)
 
-    def gather(i):
-        relay_vertex(i)
-
-        @pl.when(i == 3)
-        def _():
-            d1(core, 0).start()
-
-        @pl.when(i == 6)
-        def _():
-            d1(core, 1).start()
-            early(2)
-
-        @pl.when(i >= 1)
-        def _():
-            share(i - 1)
-            relay_bubbled(i - 1)
-
-        @pl.when(i == 4)
-        def _():
-            group_arrives(0)
-
-        @pl.when((i == 4) | (i == 5))
-        def _():
-            early(i - 4)
-
-    loop(CHUNKS, gather)
-    share(CHUNKS - 1)
-
-    @pl.when(yh == yl)
-    def _():
-        pl.semaphore_signal(go, inc=1, device_id=beside, device_id_type=MESH)
-
-    loop(2, lambda n: finish(0, n))
-
-    @pl.when(yh != yl)
-    def _():
-        pl.semaphore_wait(go, 1)
-
-    early(3)
-
-    def step(s):
-        @pl.when(s == 0)
-        def _():
-            group_arrives(1)
-
-        @pl.when(s == 1)
-        def _():
-            relay_bubbled(CHUNKS - 1)
-
-        @pl.when(s < CHUNKS)
-        def _():
-            multiply(1, s)
-
-        @pl.when((s >= 1) & (s < 4))
-        def _():
-            early(s + 3)
-
-        @pl.when((s < 2) | ((s >= 3) & (s < 6)))
-        def _():
-            finish(0, jnp.where(s < 2, s + 2, s + 1))
-
-        @pl.when((s >= 2) & (s < CHUNKS + 2))
-        def _():
-            finish(1, s - 2)
-            write(s - 2)
-
-        @pl.when(s >= 5)
-        def _():
-            place(s - 5)
-
-    loop(CHUNKS + 5, step)
-
     def sent(ref, semaphore):
         remote(ref, ref, semaphore, load_sem.at[0], partner).wait_send()
 
-    sent(panel.at[own, :, half(core)], t1_s.at[0])
-    sent(panel.at[2, :, half(core)], t2_s.at[0])
-    sent(panel.at[yh, :, half(core)], d1_s.at[0])
-    sent(panel.at[other, :, half(core)], d2_s.at[0])
+    def pass_on(i):
+        @pl.when(jnp.logical_not(end))
+        def _():
+            t1_arrives(i).wait_recv()
+            share(yh, i).start()
+
+        t2_arrives(i).wait_recv()
+        share(other, i).start()
+
+    def release():
+        @pl.when(end)
+        def _():
+            pl.semaphore_wait(go, 1)
+            loop(HELD, lambda n: c(0, n).start())
+
+        @pl.when(jnp.logical_not(end))
+        def _():
+            sent(mine, t_s.at[0])
+            pl.semaphore_signal(go, inc=1, device_id=beside, device_id_type=MESH)
+
+    def gather(i):
+        @pl.when(i == CHUNKS - 1)
+        def _():
+            release()
+
+        pass_on(i)
+
+        @pl.when((i < 2) | (i == 3) | (i == 4) | (i == 6))
+        def _():
+            relay_bubbled(jnp.where(i < 2, i, jnp.where(i < 5, i - 1, 4)))
+
+        @pl.when(i == 4)
+        def _():
+            group_arrives(0)
+            early(0)
+
+        @pl.when(i >= 4)
+        def _():
+            early(i - 3)
+
+    loop(CHUNKS, gather)
+    group_arrives(1)
+
+    def step(t):
+        late = jnp.where(t == 2, 4, jnp.where(t == 5, 5, 6))
+
+        @pl.when((t == 2) | (t == 5) | (t == 6))
+        def _():
+            early(late)
+            multiply(1, late)
+
+        @pl.when(t < 2)
+        def _():
+            loop(2, lambda n: multiply(1, 2 * t + n))
+
+        zero = (t < 4) | (t == 8) | (t == 10) | (t == 12)
+
+        @pl.when(zero)
+        def _():
+            finish(0, jnp.where(t < 4, t, t // 2))
+
+        @pl.when(jnp.logical_not(zero) & (t < 14))
+        def _():
+            n = jnp.where(t < 8, t - 4, (t - 1) // 2)
+            finish(1, n)
+            write(n)
+
+        @pl.when((t == 1) | (t == 3))
+        def _():
+            relay_bubbled(jnp.where(t == 1, 5, 6))
+
+        @pl.when(t >= 11)
+        def _():
+            place(t - 11)
+
+    loop(CHUNKS + 11, step)
+
+    @pl.when(end)
+    def _():
+        sent(mine, t_s.at[0])
+
+    @pl.when(jnp.logical_not(end))
+    def _():
+        sent(mine, t_s.at[1])
+
+    sent(panel.at[:, :, half(core)], d_s.at[0])
     for way in (0, 1):
         sent(bub.at[:, pl.ds(pl.multiple_of(x * H, H), H)], bx_s.at[way])
         start = lax.rem(x + (3, 1)[way], 4) * H + way * (H // 2)
@@ -443,7 +463,8 @@
         scratch_shapes=[
             pltpu.VMEM((D, D), BF),
             pltpu.VMEM((D, D), BF),
-            pltpu.VMEM((3, D, 2 * D), BF),
+            pltpu.VMEM((2, D, 2 * D), BF),
+            pltpu.VMEM((D, D), BF),
             pltpu.VMEM((D, D), BF),
             pltpu.VMEM((D, D), BF),
             pltpu.VMEM((2, H), BF),
@@ -458,14 +479,11 @@
             pltpu.VMEM((CHUNKS, G, 2 * T, W), BF),
             dma((4,)),
             dma((2,)),
+            dma((2,)),
+            dma((CHUNKS,)),
+            dma((CHUNKS,)),
             dma((1,)),
-            dma((PIECES,)),
-            dma((1,)),
-            dma((PIECES,)),
-            dma((1,)),
-            dma((2,)),
-            dma((1,)),
-            dma((2,)),
+            dma((2, 2)),
             dma((2,)),
             dma((2, CHUNKS)),
             dma((2,)),

time: 102 us -> 91.1 us (0.89)
  Pallas kernels: 97.4 us -> 87.2 us
    pallas_call x1, Pallas kernels: 97.4 us -> 87.2 us  [shards(): pl.pallas_call(kernel, out_shape=[pltpu.VMEM((D, D), BF)] * 2, in_specs=[...]
where the time goes in v3:
time: 91.1 us; the launch traced here: 90.1 us
  Pallas kernels  87.2 us (96%)
  local copies, waits for them, and re-layouts  2.31 us (3%)
    pallas_call x1, Pallas kernels, shards(): pl.pallas_call(kernel, out_shape=[pltpu.VMEM((D, D), BF)] * 2, in_specs=[...  87.2 us
    unnamed x2, local copies, waits for them, and re-layouts  2.31 us

profile of v3, /device:TPU:1, one launch (start us, length us, event | category | flops | bytes accessed | tf_op | source)
XLA Modules:
  0.0 90.1 jit_solution(11070987802817911597)
XLA Ops:
  0.6 87.2 %shard_map.59 = (bf16[896,896]{1,0:T(8,128)(2,1)S(1)}, bf16[896,896]{1,0:T(8,128)(2,1)S(1)}) custom-call(bf16[896,896]{1,0:T(8,128)(2,1)} %bitcast.7, bf16[2,448]{1,0:T(2,128)(2,1)} %bitcast.9, bf16[896,896]{1,0:T(8,128)(2,1)} %bitcast.8, s32[8,64]{1,0:T(8,128)} %cross_map.1), custom_call_target="tpu_custom_call" | custom-call | flops 11509170176 | bytes 6422528 | tf_op jit(solution)/shard_map/pallas_call | solution.py:453
  87.8 1.2 %copy.8 = bf16[1,2,448,896]{3,2,1,0:T(8,128)(2,1)} copy(bf16[1,2,448,896]{3,2,1,0:T(8,128)(2,1)S(1)} %bitcast.6) | data formatting | bytes 3211264
  89.0 1.2 %copy.9 = bf16[1,2,448,896]{3,2,1,0:T(8,128)(2,1)} copy(bf16[1,2,448,896]{3,2,1,0:T(8,128)(2,1)S(1)} %bitcast.5) | data formatting | bytes 3211264

commit v4 on v3

--- a/solution.py
+++ b/solution.py
@@ -15,7 +15,7 @@
 HELD = 3
 AHEAD = 2
 E = 8
-GROUPS = ((0, 4), (4, 3))
+GROUPS = ((0, 2), (2, 2), (4, 3))
 BF = jnp.bfloat16
 F32 = jnp.float32
 
@@ -120,7 +120,7 @@
         return remote(ref, ref, t_s.at[0], t2_r.at[i], across)
 
     def group_of(i):
-        return jnp.where(i < GROUPS[1][0], 0, 1)
+        return jnp.where(i < GROUPS[1][0], 0, jnp.where(i < GROUPS[2][0], 1, 2))
 
     def group_rows(group):
         first, count = GROUPS[group]
@@ -264,7 +264,7 @@
     def multiply(group, n):
         product(group, n, other, part_out)
         product(group, n, yh, kept)
-        if group:
+        if group == 2:
             c(group, n).start()
         else:
 
@@ -314,7 +314,7 @@
 
     def place(n):
         columns = pl.ds(pl.multiple_of(n * W, W), W)
-        for group in (0, 1):
+        for group in (0, 1, 2):
             cross_arrives(group, n).wait_recv()
         settled[...] = cross_in[n]
         blocks = [settled[comes[block]].astype(F32) for block in range(G)]
@@ -347,6 +347,7 @@
     def early(n):
         bubbled_arrives(n)
         multiply(0, n)
+        multiply(1, n)
 
     def sent(ref, semaphore):
         remote(ref, ref, semaphore, load_sem.at[0], partner).wait_send()
@@ -364,7 +365,12 @@
         @pl.when(end)
         def _():
             pl.semaphore_wait(go, 1)
-            loop(HELD, lambda n: c(0, n).start())
+
+            def start(n):
+                c(0, n).start()
+                c(1, n).start()
+
+            loop(HELD, start)
 
         @pl.when(jnp.logical_not(end))
         def _():
@@ -382,9 +388,14 @@
         def _():
             relay_bubbled(jnp.where(i < 2, i, jnp.where(i < 5, i - 1, 4)))
 
+        @pl.when(i == CHUNKS - 1)
+        def _():
+            finish(0, 0)
+
         @pl.when(i == 4)
         def _():
             group_arrives(0)
+            group_arrives(1)
             early(0)
 
         @pl.when(i >= 4)
@@ -392,41 +403,49 @@
             early(i - 3)
 
     loop(CHUNKS, gather)
-    group_arrives(1)
+    finish(1, 0)
+    group_arrives(2)
 
     def step(t):
         late = jnp.where(t == 2, 4, jnp.where(t == 5, 5, 6))
-
-        @pl.when((t == 2) | (t == 5) | (t == 6))
+        zero = (t < 3) | (t == 7) | (t == 9) | (t == 11)
+
+        @pl.when((t == 5) | (t == 6))
         def _():
             early(late)
-            multiply(1, late)
-
-        @pl.when(t < 2)
-        def _():
-            loop(2, lambda n: multiply(1, 2 * t + n))
-
-        zero = (t < 4) | (t == 8) | (t == 10) | (t == 12)
+            multiply(2, late)
+
+        @pl.when(t < 3)
+        def _():
+            multiply(2, t)
+
+        @pl.when((t == 1) | (t == 3))
+        def _():
+            relay_bubbled(jnp.where(t == 1, 5, 6))
 
         @pl.when(zero)
         def _():
-            finish(0, jnp.where(t < 4, t, t // 2))
-
-        @pl.when(jnp.logical_not(zero) & (t < 14))
-        def _():
-            n = jnp.where(t < 8, t - 4, (t - 1) // 2)
+            n = jnp.where(t < 3, t + 1, (t + 1) // 2)
+            finish(0, n)
             finish(1, n)
+
+        @pl.when(t == 2)
+        def _():
+            multiply(2, 3)
+            early(4)
+            multiply(2, 4)
+
+        @pl.when(jnp.logical_not(zero) & (t < 13))
+        def _():
+            n = jnp.where(t < 7, t - 3, t // 2)
+            finish(2, n)
             write(n)
 
-        @pl.when((t == 1) | (t == 3))
-        def _():
-            relay_bubbled(jnp.where(t == 1, 5, 6))
-
-        @pl.when(t >= 11)
-        def _():
-            place(t - 11)
-
-    loop(CHUNKS + 11, step)
+        @pl.when(t >= 10)
+        def _():
+            place(t - 10)
+
+    loop(CHUNKS + 10, step)
 
     @pl.when(end)
     def _():
@@ -483,15 +502,15 @@
             dma((CHUNKS,)),
             dma((CHUNKS,)),
             dma((1,)),
-            dma((2, 2)),
+            dma((2, 3)),
             dma((2,)),
             dma((2, CHUNKS)),
             dma((2,)),
             dma((2, CHUNKS)),
             dma((1,)),
-            dma((2, CHUNKS)),
+            dma((3, CHUNKS)),
             dma((1,)),
-            dma((2, CHUNKS)),
+            dma((3, CHUNKS)),
             pltpu.SemaphoreType.REGULAR,
         ],
         compiler_params=pltpu.CompilerParams(

time: 91.1 us -> 89.7 us (0.985)
  no operation moved by 1% of the time
where the time goes in v4:
time: 89.7 us; the launch traced here: 89.4 us
  Pallas kernels  86.5 us (96%)
  local copies, waits for them, and re-layouts  2.31 us (3%)
    pallas_call x1, Pallas kernels, shards(): pl.pallas_call(kernel, out_shape=[pltpu.VMEM((D, D), BF)] * 2, in_specs=[...  86.5 us
    unnamed x2, local copies, waits for them, and re-layouts  2.31 us

profile of v4, /device:TPU:1, one launch (start us, length us, event | category | flops | bytes accessed | tf_op | source)
XLA Modules:
  0.0 89.4 jit_solution(15326727200759909858)
XLA Ops:
  0.6 86.5 %shard_map.59 = (bf16[896,896]{1,0:T(8,128)(2,1)S(1)}, bf16[896,896]{1,0:T(8,128)(2,1)S(1)}) custom-call(bf16[896,896]{1,0:T(8,128)(2,1)} %bitcast.7, bf16[2,448]{1,0:T(2,128)(2,1)} %bitcast.9, bf16[896,896]{1,0:T(8,128)(2,1)} %bitcast.8, s32[8,64]{1,0:T(8,128)} %cross_map.1), custom_call_target="tpu_custom_call" | custom-call | flops 11509170176 | bytes 6422528 | tf_op jit(solution)/shard_map/pallas_call | solution.py:472
  87.1 1.2 %copy.8 = bf16[1,2,448,896]{3,2,1,0:T(8,128)(2,1)} copy(bf16[1,2,448,896]{3,2,1,0:T(8,128)(2,1)S(1)} %bitcast.6) | data formatting | bytes 3211264
  88.3 1.2 %copy.9 = bf16[1,2,448,896]{3,2,1,0:T(8,128)(2,1)} copy(bf16[1,2,448,896]{3,2,1,0:T(8,128)(2,1)S(1)} %bitcast.5) | data formatting | bytes 3211264

commit v5 on v4

--- a/solution.py
+++ b/solution.py
@@ -13,6 +13,7 @@
 G = 8
 T = 56
 HELD = 3
+FAR_FIRST = (4, 3, 5, 2, 6, 1, 7, 0)
 AHEAD = 2
 E = 8
 GROUPS = ((0, 2), (2, 2), (4, 3))
@@ -288,7 +289,7 @@
                     start = i * W + part * (W // 2) + block * E
                     pieces.append(value[start : start + E])
             turn[block, high] = jnp.concatenate(pieces, axis=0).astype(BF)
-        for step in range(G):
+        for step in FAR_FIRST:
             if step:
                 cross_out[n, step, high] = turn[goes[step], high]
                 cross(group, n, step).start()
@@ -465,6 +466,17 @@
     for which in (0, 1):
         source, target = ((updated, updated_out), (crossed, crossed_out))[which]
         pltpu.make_async_copy(source, target, store_sem.at[which]).wait()
+
+
+def hand_over(updated, crossed, updated_out, crossed_out, sem):
+    copies = [
+        pltpu.make_async_copy(updated, updated_out, sem.at[0]),
+        pltpu.make_async_copy(crossed, crossed_out, sem.at[1]),
+    ]
+    for copy in copies:
+        copy.start()
+    for copy in copies:
+        copy.wait()
 
 
 def shards(vertex, bubble, previous, cross_map):
@@ -518,6 +530,15 @@
         ),
         cost_estimate=pl.CostEstimate(flops=8 * H * 4 * D * D, bytes_accessed=8 * D * D, transcendentals=0),
     )(vertex.reshape(D, D), bubble.reshape(2, H), previous.reshape(D, D), cross_map)
+    updated, crossed = pl.pallas_call(
+        hand_over,
+        out_shape=[jax.ShapeDtypeStruct((D, D), BF)] * 2,
+        in_specs=[pl.BlockSpec(memory_space=pl.ANY)] * 2,
+        out_specs=[pl.BlockSpec(memory_space=pl.ANY)] * 2,
+        scratch_shapes=[pltpu.SemaphoreType.DMA((2,))],
+        compiler_params=pltpu.CompilerParams(vmem_limit_bytes=4 * 2**20),
+        cost_estimate=pl.CostEstimate(flops=0, bytes_accessed=8 * D * D, transcendentals=0),
+    )(updated, crossed)
     return updated.reshape(1, 2, H, D), crossed.reshape(1, 2, H, D)
 
 

time: 89.7 us -> 88.9 us (level)
  local copies, waits for them, and re-layouts: 2.31 us -> 0 us
    unnamed x2 -> x0, local copies, waits for them, and re-layouts: 2.31 us -> none
    pallas_call x0 -> x1, Pallas kernels: none -> 1.7 us  [shards(): pl.pallas_call(hand_over, out_shape=[jax.ShapeDtypeStruct((D, D), BF)] *...]
where the time goes in v5:
time: 88.9 us; the launch traced here: 88 us
  Pallas kernels  87.3 us (98%)
    pallas_call x1, Pallas kernels, shards(): pl.pallas_call(kernel, out_shape=[pltpu.VMEM((D, D), BF)] * 2, in_specs=[...  85.6 us

profile of v5, /device:TPU:1, one launch (start us, length us, event | category | flops | bytes accessed | tf_op | source)
XLA Modules:
  0.0 88.0 jit_solution(5080656461816856361)
XLA Ops:
  0.6 85.6 %shard_map.59 = (bf16[896,896]{1,0:T(8,128)(2,1)S(1)}, bf16[896,896]{1,0:T(8,128)(2,1)S(1)}) custom-call(bf16[896,896]{1,0:T(8,128)(2,1)} %bitcast.5, bf16[2,448]{1,0:T(2,128)(2,1)} %bitcast.9, bf16[896,896]{1,0:T(8,128)(2,1)} %bitcast.6, s32[8,64]{1,0:T(8,128)} %cross_map.1), custom_call_target="tpu_custom_call" | custom-call | flops 11509170176 | bytes 6422528 | tf_op jit(solution)/shard_map/pallas_call | solution.py:484
  86.3 1.7 %shard_map.60 = (bf16[896,896]{1,0:T(8,128)(2,1)}, bf16[896,896]{1,0:T(8,128)(2,1)}) custom-call(bf16[896,896]{1,0:T(8,128)(2,1)S(1)} %get-tuple-element.6.updated, bf16[896,896]{1,0:T(8,128)(2,1)S(1)} %get-tuple-element.7.crossed), custom_call_target="tpu_custom_call" | custom-call | bytes 6422528 | tf_op jit(solution)/shard_map/pallas_call | solution.py:533

commit v6 on v5

--- a/solution.py
+++ b/solution.py
@@ -34,7 +34,6 @@
     mine,
     raw,
     prev,
-    diag,
     cmap,
     bub,
     kept,
@@ -84,8 +83,7 @@
 
     load_a = pltpu.make_async_copy(vertex, raw, load_sem.at[0])
     load_p = pltpu.make_async_copy(previous, prev, load_sem.at[1])
-    load_d = pltpu.make_async_copy(bubble, diag, load_sem.at[2])
-    load_m = pltpu.make_async_copy(cross_map, cmap, load_sem.at[3])
+    load_m = pltpu.make_async_copy(cross_map, cmap, load_sem.at[2])
     load_a.start()
 
     barrier = pltpu.get_barrier_semaphore()
@@ -182,7 +180,7 @@
         lax.fori_loop(0, count, run, 0)
 
     load_a.wait()
-    for load in (load_p, load_d, load_m):
+    for load in (load_p, load_m):
         load.start()
 
     def arrange(n):
@@ -214,10 +212,10 @@
         loop(CHUNKS, lambda i: t_far(i).start())
         loop(CHUNKS, lambda i: t_middle(i).start())
 
-    for load in (load_p, load_d, load_m):
+    for load in (load_p, load_m):
         load.wait()
-    first = jnp.broadcast_to(diag[0:1, :].astype(F32), (W, H)).T
-    second = jnp.broadcast_to(diag[1:2, :].astype(F32), (W, H)).T
+    first = jnp.broadcast_to(bubble[0:1, :].astype(F32), (W, H)).T
+    second = jnp.broadcast_to(bubble[1:2, :].astype(F32), (W, H)).T
 
     def make_bubbled(n):
         columns = pl.ds(pl.multiple_of(n * W, W), W)
@@ -486,7 +484,7 @@
         out_shape=[pltpu.VMEM((D, D), BF)] * 2,
         in_specs=[
             pl.BlockSpec(memory_space=pltpu.HBM),
-            pl.BlockSpec(memory_space=pltpu.HBM),
+            pl.BlockSpec(memory_space=pltpu.VMEM),
             pl.BlockSpec(memory_space=pltpu.HBM),
             pl.BlockSpec(memory_space=pltpu.HBM),
         ],
@@ -498,7 +496,6 @@
             pltpu.VMEM((D, D), BF),
             pltpu.VMEM((D, D), BF),
             pltpu.VMEM((D, D), BF),
-            pltpu.VMEM((2, H), BF),
             pltpu.SMEM((G, G * G), jnp.int32),
             pltpu.VMEM((CHUNKS, 4 * H, 2 * W), BF),
             pltpu.VMEM((CHUNKS, D, W), F32),
@@ -508,7 +505,7 @@
             pltpu.VMEM((G, 2 * T, W), BF),
             pltpu.VMEM((CHUNKS, G, 2 * T, W), BF),
             pltpu.VMEM((CHUNKS, G, 2 * T, W), BF),
-            dma((4,)),
+            dma((3,)),
             dma((2,)),
             dma((2,)),
             dma((CHUNKS,)),

time: 88.9 us -> 89.5 us (level)
  no operation moved by 1% of the time
where the time goes in v6:
time: 89.5 us; the launch traced here: 88.6 us
  Pallas kernels  88 us (98%)
    pallas_call x1, Pallas kernels, shards(): pl.pallas_call(kernel, out_shape=[pltpu.VMEM((D, D), BF)] * 2, in_specs=[...  86.3 us

profile of v6, /device:TPU:1, one launch (start us, length us, event | category | flops | bytes accessed | tf_op | source)
XLA Modules:
  0.0 88.6 jit_solution(10431578605221253072)
XLA Ops:
  0.6 86.3 %shard_map.59 = (bf16[896,896]{1,0:T(8,128)(2,1)S(1)}, bf16[896,896]{1,0:T(8,128)(2,1)S(1)}) custom-call(bf16[896,896]{1,0:T(8,128)(2,1)} %bitcast.5, bf16[2,448]{1,0:T(2,128)(2,1)} %bitcast.9, bf16[896,896]{1,0:T(8,128)(2,1)} %bitcast.6, s32[8,64]{1,0:T(8,128)} %cross_map.1), custom_call_target="tpu_custom_call" | custom-call | flops 11509170176 | bytes 6422528 | tf_op jit(solution)/shard_map/pallas_call | solution.py:482
  86.9 1.7 %shard_map.60 = (bf16[896,896]{1,0:T(8,128)(2,1)}, bf16[896,896]{1,0:T(8,128)(2,1)}) custom-call(bf16[896,896]{1,0:T(8,128)(2,1)S(1)} %get-tuple-element.6.updated, bf16[896,896]{1,0:T(8,128)(2,1)S(1)} %get-tuple-element.7.crossed), custom_call_target="tpu_custom_call" | custom-call | bytes 6422528 | tf_op jit(solution)/shard_map/pallas_call | solution.py:530

commit v7 on v5

--- a/solution.py
+++ b/solution.py
@@ -89,10 +89,11 @@
     load_a.start()
 
     barrier = pltpu.get_barrier_semaphore()
+    for step in FAR_FIRST[:-1]:
+        pl.semaphore_signal(barrier, inc=1, device_id=(lax.rem(z + step, G), row, col), device_id_type=MESH)
     for device in (right, left, beside, across, sibling, partner):
         pl.semaphore_signal(barrier, inc=1, device_id=device, device_id_type=MESH)
-    for step in range(1, G):
-        pl.semaphore_signal(barrier, inc=1, device_id=(lax.rem(z + step, G), row, col), device_id_type=MESH)
+
 
     def half(which):
         return pl.ds(pl.multiple_of(which * D, D), D)
@@ -211,8 +212,8 @@
 
     @pl.when(jnp.logical_not(end))
     def _():
+        loop(CHUNKS, lambda i: t_middle(i).start())
         loop(CHUNKS, lambda i: t_far(i).start())
-        loop(CHUNKS, lambda i: t_middle(i).start())
 
     for load in (load_p, load_d, load_m):
         load.wait()

time: 88.9 us -> 88.8 us (level)
  no operation moved by 1% of the time
where the time goes in v7:
time: 88.8 us; the launch traced here: 88 us
  Pallas kernels  87.4 us (98%)
    pallas_call x1, Pallas kernels, shards(): pl.pallas_call(kernel, out_shape=[pltpu.VMEM((D, D), BF)] * 2, in_specs=[...  85.7 us

profile of v7, /device:TPU:1, one launch (start us, length us, event | category | flops | bytes accessed | tf_op | source)
XLA Modules:
  0.0 88.0 jit_solution(17980433140424584043)
XLA Ops:
  0.6 85.7 %shard_map.59 = (bf16[896,896]{1,0:T(8,128)(2,1)S(1)}, bf16[896,896]{1,0:T(8,128)(2,1)S(1)}) custom-call(bf16[896,896]{1,0:T(8,128)(2,1)} %bitcast.5, bf16[2,448]{1,0:T(2,128)(2,1)} %bitcast.9, bf16[896,896]{1,0:T(8,128)(2,1)} %bitcast.6, s32[8,64]{1,0:T(8,128)} %cross_map.1), custom_call_target="tpu_custom_call" | custom-call | flops 11509170176 | bytes 6422528 | tf_op jit(solution)/shard_map/pallas_call | solution.py:485
  86.3 1.7 %shard_map.60 = (bf16[896,896]{1,0:T(8,128)(2,1)}, bf16[896,896]{1,0:T(8,128)(2,1)}) custom-call(bf16[896,896]{1,0:T(8,128)(2,1)S(1)} %get-tuple-element.6.updated, bf16[896,896]{1,0:T(8,128)(2,1)S(1)} %get-tuple-element.7.crossed), custom_call_target="tpu_custom_call" | custom-call | bytes 6422528 | tf_op jit(solution)/shard_map/pallas_call | solution.py:534
